TPU v7x, 32 devices: a whole 2x2x4 slice. The times are simulated.
32 devices in a mesh: view: 4 (over z), seg: 8 (over y, x, core).
Axes of the slice: x: 2, y: 2, z: 4, core: 2. Of those that a mesh axis runs over, the one named last changes fastest.
Arguments:
- features: bfloat16 [32, 1369, 1024], P(('view', 'seg')), may hold values from -6 to 6
- block_ids: int32 [32, 8, 2], P(('view', 'seg')), may hold values from 0 to 32, as said below
- patch_rows: int32 [32, 8, 2, 32], P(('view', 'seg')), may hold values from 0 to 1368
- lift_weights: bfloat16 [32, 8, 2, 64, 32], P(('view', 'seg')), may hold values from 0 to 0.5
- coords: int32 [4, 8, 3, 512], P('view', 'seg'), may hold values from 0 to 127, as said below
- w_in: float32 [1024, 768], replicated, may hold values from -0.1875 to 0.1875
- w_query: bfloat16 [768, 768], replicated, may hold values from -1 to 1
- w_key: bfloat16 [768, 768], replicated, may hold values from -1 to 1
- w_value: bfloat16 [768, 768], replicated, may hold values from -0.21875 to 0.21875
- w_out: bfloat16 [768, 768], replicated, may hold values from -0.21875 to 0.21875
- w_up: bfloat16 [768, 3072], replicated, may hold values from -0.21875 to 0.21875
- w_down: bfloat16 [3072, 768], replicated, may hold values from -0.109375 to 0.109375
Outputs:
- encoded: bfloat16 [4, 8, 512, 768], P('view', 'seg')
Inputs may be any that keep to these rules, and one draw needn't show every extreme that they name: In each row block_ids[j, s] the live entries (below 32) come first, are distinct and number 1 to 2; the others equal 32. All rows of one destination segment are full. The value 4 * 8 - 1 never occurs. `coords`: the three coordinates of distinct voxels of a 128-cube; their Morton codes rise strictly with the voxel index.
All inputs are finite; a program needn't handle non-finite values.
Results may differ from a plain program's by a relative error of at most 0.007.
Values may be sent and summed in bfloat16 or wider, within the bound.
A program may use at most 128 MiB of HBM per device.

v0:
```python
import functools
import math

import jax
import jax.numpy as jnp
from jax import lax
from jax.experimental import pallas as pl
from jax.experimental.pallas import tpu as pltpu
from jax.sharding import PartitionSpec as P

HEAD_DIM = 64
MESH = pl.DeviceIdType.MESH
F32 = jnp.float32
BF16 = jnp.bfloat16
CW = 128
ID_ROWS = 16
FF_STEP = 512
VMEM_LIMIT = 56 * 1024 * 1024


def normalize(values):
    average = jnp.mean(values, axis=-1, keepdims=True)
    centred = values - average
    spread = jnp.mean(centred * centred, axis=-1, keepdims=True)
    return (centred * lax.rsqrt(spread + 1e-05)).astype(BF16)


def whole_kernel(
    V, G, cfg,
    features, patch_rows, block_ids, lift_weights, coords, w_in,
    w_query, w_key, w_value, w_out, w_up, w_down,
    encoded,
    wmsg, sb, pp, wm, sums_out, sums_in, tal_out, tal_in, stream, halo, vq, vk, vv, vo, bias,
    asend, arecv, zsend, zrecv, ssend, srecv, hsend, hrecv, lsem,
):
    KS, BP, BLK, QB, CC = cfg
    rows = QB * BLK
    half = BLK // 2
    width = stream.shape[1]
    total = rows + BLK
    me_v = lax.axis_index("view")
    me_g = lax.axis_index("seg")
    outer = (me_v == 0) | (me_v == V - 1)
    middle = jnp.logical_not(outer)
    inner_of = jnp.where(me_v == 0, 1, V - 2)
    outer_of = jnp.where(me_v == 1, 0, V - 1)
    other = V - 1 - me_v
    far = V - 1 - outer_of
    flat = me_v * G + me_g
    nxt = lax.rem(flat + 1, V * G)
    prv = lax.rem(flat + V * G - 1, V * G)
    nxt_id = (nxt // G, lax.rem(nxt, G))
    prv_id = (prv // G, lax.rem(prv, G))

    loads = [
        pltpu.make_async_copy(a, b, lsem.at[i + 2])
        for i, (a, b) in enumerate([(w_query, vq), (w_key, vk), (w_value, vv), (w_out, vo)])
    ]

    barrier = pltpu.get_barrier_semaphore()

    def remote(src, dst, s, r, dev):
        return pltpu.make_async_remote_copy(
            src_ref=src, dst_ref=dst, send_sem=s, recv_sem=r,
            device_id=dev, device_id_type=MESH,
        )

    def seg_copy(cc, off):
        peer = lax.rem(me_g + off, G)
        if cc == CC:
            src, dst = wmsg.at[peer], wm.at[me_v, me_g]
        else:
            src, dst = sb.at[cc, peer], pp.at[me_v, cc, me_g]
        return remote(src, dst, asend.at[cc, off], arecv.at[cc, off], (me_v, peer))

    def seg_wait_recv(cc, off):
        src_g = lax.rem(me_g + G - off, G)
        buf = wm.at[me_v, src_g] if cc == CC else pp.at[me_v, cc, src_g]
        remote(buf, buf, asend.at[cc, off], arecv.at[cc, off], (me_v, src_g)).wait_recv()

    def view_copy(z, cc, kind, dev_v):
        buf = wm.at[z] if cc == CC else pp.at[z, cc]
        return remote(buf, buf, zsend.at[kind, cc], zrecv.at[kind, cc], (dev_v, me_g))

    def sum_copy(cc):
        if cc == CC:
            return remote(tal_out, tal_in, ssend.at[cc], srecv.at[cc], (outer_of, me_g))
        return remote(sums_out.at[cc], sums_in.at[cc], ssend.at[cc], srecv.at[cc], (outer_of, me_g))

    def to_view(cc):
        for off in range(1, G):
            seg_wait_recv(cc, off)

        @pl.when(outer)
        def _():
            view_copy(me_v, cc, 0, inner_of).start()

        @pl.when(middle)
        def _():
            view_copy(me_v, cc, 1, other).start()

    lane = lax.broadcasted_iota(jnp.int32, (1, 2 * KS), 1)

    def send_patches(feat, win, gathered):
        load_feat = pltpu.make_async_copy(features.at[0], feat, lsem.at[0])
        load_win = pltpu.make_async_copy(w_in, win, lsem.at[1])
        load_feat.start()
        load_win.start()
        def greet(dev):
            pl.semaphore_signal(barrier, inc=1, device_id=dev, device_id_type=MESH)

        for off in range(1, G):
            greet((me_v, lax.rem(me_g + off, G)))
        greet(nxt_id)
        greet(prv_id)

        @pl.when(outer)
        def _():
            greet((inner_of, me_g))

        @pl.when(middle)
        def _():
            greet((outer_of, me_g))
            greet((other, me_g))

        slot_of = lax.rem(lane, KS) // BP
        marks = block_ids[0].astype(F32)
        for s in range(G):
            pieces = [lift_weights[0, s, c].astype(F32) for c in range(KS // BP)]
            turned = jnp.transpose(jnp.concatenate(pieces, axis=0))
            folded = jnp.concatenate([turned[:half], turned[half:]], axis=1)
            row = jnp.zeros((1, 2 * KS), F32)
            for c in range(KS // BP):
                row = jnp.where(slot_of == c, marks[c:c + 1, s:s + 1], row)
            wmsg[s] = jnp.concatenate(
                [folded, jnp.broadcast_to(row, (ID_ROWS, 2 * KS))], axis=0
            ).astype(BF16)

        pl.semaphore_wait(barrier, G + 1 + jnp.where(outer, 1, 2))

        for off in range(1, G):
            seg_copy(CC, off).start()
        wm[me_v, me_g] = wmsg[me_g]

        patches = feat.shape[0]
        picks = jnp.concatenate([patch_rows[0, s].astype(F32) for s in range(G)], axis=0)
        picks = jnp.transpose(picks)
        load_feat.wait()
        step = min(256, G * KS)
        for at in range(0, G * KS, step):
            chosen = jnp.concatenate(
                [picks[:, n:n + 1] for n in range(at // BP, (at + step) // BP)], axis=0
            ).astype(jnp.int32)
            hot = (lax.broadcasted_iota(jnp.int32, (step, patches), 1) == chosen).astype(F32).astype(BF16)
            gathered[at:at + step, :] = jnp.dot(hot, feat[...], preferred_element_type=F32).astype(BF16)

        load_win.wait()
        to_view(CC)
        for group in range(CC // 2):
            full = win[:, group * 2 * CW:(group + 1) * 2 * CW]
            high = full.astype(BF16)
            low = (full - high.astype(F32)).astype(BF16)
            rows_all = gathered[...]
            part = jnp.dot(rows_all, high, preferred_element_type=F32)
            part = part + jnp.dot(rows_all, low, preferred_element_type=F32)
            for side in range(2):
                cc = 2 * group + side
                sb[cc] = part[:, side * CW:(side + 1) * CW].astype(BF16).reshape(G, KS, CW)
                for off in range(1, G):
                    seg_copy(cc, off).start()
                pp[me_v, cc, me_g] = sb[cc, me_g]
            if group > 0:
                to_view(2 * group - 2)
                to_view(2 * group - 1)
        to_view(CC - 2)
        to_view(CC - 1)

    channels = w_in.shape[0]
    pl.run_scoped(
        send_patches,
        pltpu.VMEM(features.shape[1:], BF16),
        pltpu.VMEM((channels, width), F32),
        pltpu.VMEM((G * KS, channels), BF16),
    )
    for load in loads:
        load.start()

    order = [CC] + list(range(CC))
    lane_low = lane < KS

    freq_iota = lax.broadcasted_iota(jnp.int32, (1, CW), 1).astype(F32)
    freq = jnp.exp(-math.log(10000.0) * freq_iota / CW)
    spots = [coords[0, a].astype(F32) for a in range(coords.shape[1])]
    spots = jnp.concatenate(spots + [jnp.zeros((8 - len(spots), rows), F32)], axis=0)
    spots = jnp.transpose(spots)
    for cc in range(CC):
        angles = spots[:, cc // 2:cc // 2 + 1] * freq
        stream[:, cc * CW:(cc + 1) * CW] = jnp.sin(angles) if cc % 2 == 0 else jnp.cos(angles)
    span = 2 * BLK
    groups = [(at, min(span, total - at), min(at, total - span)) for at in range(0, total, span)]
    for at, size, kat in groups:
        row_win = (lax.broadcasted_iota(jnp.int32, (size, span), 0) + at) // BLK
        col_win = (lax.broadcasted_iota(jnp.int32, (size, span), 1) + kat) // BLK
        bias[at:at + size, :] = jnp.where(row_win == col_win, 0.0, -1e30)

    def add_up(am):
        def build(slot, z, quarter):
            tally = jnp.zeros((QB, 1), F32)
            base = (quarter * QB).astype(F32)
            blocks = lax.broadcasted_iota(jnp.int32, (QB, 2 * KS), 0).astype(F32) + base
            for pair in range(G // 2):
                first = wm[z, 2 * pair].astype(F32)
                second = wm[z, 2 * pair + 1].astype(F32)
                a, b = first[:half], second[:half]
                top = jnp.concatenate([a[:, :KS], b[:, :KS]], axis=1)
                bottom = jnp.concatenate([a[:, KS:], b[:, KS:]], axis=1)
                weights = jnp.concatenate([top, bottom], axis=0)
                ids = jnp.where(lane_low, first[half:half + 1], second[half:half + 1])
                cols = slice(pair * 2 * KS, (pair + 1) * 2 * KS)
                for blk in range(QB):
                    am[slot, z, blk * BLK:(blk + 1) * BLK, cols] = jnp.where(
                        ids == base + blk, weights, 0.0
                    ).astype(BF16)
                hits = jnp.where(ids == blocks, 1.0, 0.0)
                tally = tally + jnp.sum(hits, axis=1, keepdims=True)
            return tally * (1.0 / BP)

        def product(slot, z, cc):
            return jnp.dot(am[slot, z], pp[z, cc].reshape(G * KS, CW), preferred_element_type=F32)

        def finish(cc, summed, tally):
            cols = slice(cc * CW, (cc + 1) * CW)
            parts = []
            for blk in range(QB):
                count = jnp.maximum(tally[blk:blk + 1, :], 1.0)
                parts.append(summed[blk * BLK:(blk + 1) * BLK] / count)
            stream[:, cols] = jnp.concatenate(parts, axis=0) + stream[:, cols]

        @pl.when(outer)
        def _():
            own_tally = build(0, me_v, me_v)
            remote(tal_in, tal_in, ssend.at[CC], srecv.at[CC], (inner_of, me_g)).wait_recv()
            tally = own_tally + tal_in[:QB, 0:1].astype(F32)
            for cc in range(CC):
                mine = product(0, me_v, cc)
                remote(sums_in.at[cc], sums_in.at[cc], ssend.at[cc], srecv.at[cc], (inner_of, me_g)).wait_recv()
                finish(cc, mine + sums_in[cc].astype(F32), tally)
            for cc in order:
                view_copy(me_v, cc, 0, inner_of).wait_send()

        @pl.when(middle)
        def _():
            def pass_on(cc):
                view_copy(outer_of, cc, 0, other).wait_recv()
                view_copy(outer_of, cc, 2, other).start()

            pass_on(CC)
            pass_on(0)
            tally = build(0, me_v, me_v) + build(0, outer_of, me_v)
            for_end = build(1, me_v, outer_of)
            pass_on(1)
            view_copy(other, CC, 1, other).wait_recv()
            view_copy(far, CC, 2, other).wait_recv()
            tally = tally + build(0, other, me_v) + build(0, far, me_v)
            for_end = for_end + build(1, other, outer_of) + build(1, far, outer_of)
            tal_out[...] = jnp.concatenate(
                [jnp.broadcast_to(for_end, (QB, 128)), jnp.zeros((ID_ROWS - QB, 128), F32)], axis=0
            ).astype(BF16)
            sum_copy(CC).start()
            for cc in range(2, CC):
                pass_on(cc)
            for cc in range(CC):
                view_copy(other, cc, 1, other).wait_recv()
                early = product(1, me_v, cc) + product(1, other, cc)
                view_copy(far, cc, 2, other).wait_recv()
                sums_out[cc] = (early + product(1, far, cc)).astype(BF16)
                sum_copy(cc).start()
                summed = (
                    product(0, me_v, cc) + product(0, outer_of, cc)
                    + product(0, other, cc) + product(0, far, cc)
                )
                finish(cc, summed, tally)
            for cc in order:
                view_copy(me_v, cc, 1, other).wait_send()
                view_copy(outer_of, cc, 2, other).wait_send()
                sum_copy(cc).wait_send()

    pl.run_scoped(add_up, pltpu.VMEM((2, V, rows, G * KS), BF16))

    def transform(vup, vdown, normed, query, keys, values, mixed, hidden):
        halo[0] = normalize(stream[:half, :])
        halo[1] = normalize(stream[rows - half:, :])
        back = remote(halo.at[0], halo.at[2], hsend.at[0], hrecv.at[0], prv_id)
        ahead = remote(halo.at[1], halo.at[3], hsend.at[1], hrecv.at[1], nxt_id)
        back.start()
        ahead.start()
        load_up = pltpu.make_async_copy(w_up, vup, lsem.at[6])
        load_down = pltpu.make_async_copy(w_down, vdown, lsem.at[7])
        load_up.start()
        load_down.start()
        for at in range(0, rows, BLK):
            normed[at:at + BLK, :] = normalize(stream[at:at + BLK, :])
        query[:half, :] = jnp.zeros((half, width), BF16)
        query[half + rows:, :] = jnp.zeros((half, width), BF16)
        for load, mat, out in zip(loads[:3], (vq, vk, vv), (query, keys, values)):
            load.wait()
            out[half:half + rows, :] = jnp.dot(normed[...], mat[...], preferred_element_type=F32).astype(BF16)
        for cc in order:
            for off in range(1, G):
                seg_copy(cc, off).wait_send()
        back.wait()
        ahead.wait()
        edges = jnp.concatenate([halo[3], halo[2]], axis=0)
        for mat, out in zip((vk, vv), (keys, values)):
            edge = jnp.dot(edges, mat[...], preferred_element_type=F32).astype(BF16)
            out[:half, :] = edge[:half]
            out[half + rows:, :] = edge[half:]

        pair = 2 * HEAD_DIM
        low = lax.broadcasted_iota(jnp.int32, (1, pair), 1) < HEAD_DIM
        scale = 1.0 / math.sqrt(HEAD_DIM)
        on_low = jnp.where(low, scale, 0.0).astype(BF16)
        on_high = jnp.where(low, 0.0, scale).astype(BF16)
        ones = jnp.ones((span, pair), BF16)

        def head_step(h, carry):
            cols = pl.ds(pl.multiple_of(h * pair, pair), pair)
            q, k, v = query[:, cols], keys[:, cols], values[:, cols]
            scores = []
            for at, size, kat in groups:
                qs = q[at:at + size]
                both = jnp.concatenate([qs * on_low, qs * on_high], axis=0)
                mask = bias[at:at + size, :]
                scores.append(lax.dot_general(
                    both, k[kat:kat + span], (((1,), (1,)), ((), ())), preferred_element_type=F32,
                ) + jnp.concatenate([mask, mask], axis=0))
            block = jnp.concatenate(scores, axis=0)
            e = jnp.exp(block - jnp.max(block, axis=-1, keepdims=True)).astype(BF16)
            for at, size, kat in groups:
                right = jnp.concatenate([v[kat:kat + span], ones], axis=1)
                out = jnp.dot(e[2 * at:2 * (at + size)], right, preferred_element_type=F32)
                top, bottom = out[:size], out[size:]
                weighted = jnp.where(low, top[:, :pair], bottom[:, :pair])
                sums = jnp.where(low, top[:, pair:], bottom[:, pair:])
                mixed[at:at + size, cols] = (weighted / sums).astype(BF16)
            return carry

        lax.fori_loop(0, width // pair, head_step, 0, unroll=2)

        loads[3].wait()
        stream[...] = stream[...] + jnp.dot(
            mixed[half:half + rows, :], vo[...], preferred_element_type=F32
        )
        for at in range(0, rows, BLK):
            normed[at:at + BLK, :] = normalize(stream[at:at + BLK, :])
        load_up.wait()
        load_down.wait()
        step = hidden.shape[2]
        count = vup.shape[1] // step

        def down(i):
            stream[...] += jnp.dot(
                hidden[i % 2], vdown[i * step:(i + 1) * step, :], preferred_element_type=F32
            )

        for i in range(count):
            up = jnp.dot(normed[...], vup[:, i * step:(i + 1) * step], preferred_element_type=F32)
            if i > 0:
                down(i - 1)
            hidden[i % 2] = jax.nn.gelu(up, approximate=True).astype(BF16)
        encoded[...] = (stream[...] + jnp.dot(
            hidden[(count - 1) % 2], vdown[(count - 1) * step:, :], preferred_element_type=F32
        )).astype(BF16)

    extended = pltpu.VMEM((total, width), BF16)
    pl.run_scoped(
        transform,
        pltpu.VMEM(w_up.shape, BF16),
        pltpu.VMEM(w_down.shape, BF16),
        pltpu.VMEM((rows, width), BF16),
        extended, extended, extended, extended,
        pltpu.VMEM((2, rows, FF_STEP), BF16),
    )


def shards(
    features, block_ids, patch_rows, lift_weights, coords, w_in,
    w_query, w_key, w_value, w_out, w_up, w_down,
):
    V, G = lax.axis_size("view"), lax.axis_size("seg")
    _, _, cap, blk, bp = lift_weights.shape
    rows = coords.shape[-1]
    width = w_in.shape[1]
    KS, QB, CC, half = cap * bp, rows // blk, width // CW, blk // 2
    vmem = pl.BlockSpec(memory_space=pltpu.VMEM)
    anyspace = pl.BlockSpec(memory_space=pl.ANY)
    dma = pltpu.SemaphoreType.DMA
    encoded = pl.pallas_call(
        functools.partial(whole_kernel, V, G, (KS, bp, blk, QB, CC)),
        out_shape=jax.ShapeDtypeStruct((rows, width), BF16),
        in_specs=[anyspace] + [vmem] * 4 + [anyspace] * 7,
        out_specs=vmem,
        scratch_shapes=[
            pltpu.VMEM((G, half + ID_ROWS, 2 * KS), BF16),
            pltpu.VMEM((CC, G, KS, CW), BF16),
            pltpu.VMEM((V, CC, G, KS, CW), BF16),
            pltpu.VMEM((V, G, half + ID_ROWS, 2 * KS), BF16),
            pltpu.VMEM((CC, rows, CW), BF16),
            pltpu.VMEM((CC, rows, CW), BF16),
            pltpu.VMEM((ID_ROWS, 128), BF16),
            pltpu.VMEM((ID_ROWS, 128), BF16),
            pltpu.VMEM((rows, width), F32),
            pltpu.VMEM((4, half, width), BF16),
        ]
        + [pltpu.VMEM((width, width), BF16)] * 4
        + [
            pltpu.VMEM((rows + blk, 2 * blk), F32),
            dma((CC + 1, G)),
            dma((CC + 1, G)),
            dma((3, CC + 1)),
            dma((3, CC + 1)),
            dma((CC + 1,)),
            dma((CC + 1,)),
            dma((2,)),
            dma((2,)),
            dma((8,)),
        ],
        compiler_params=pltpu.CompilerParams(
            collective_id=0, has_side_effects=True, vmem_limit_bytes=VMEM_LIMIT
        ),
        name="voxel_block",
    )(
        features, patch_rows, jnp.transpose(block_ids, (0, 2, 1)),
        jnp.transpose(lift_weights, (0, 1, 2, 4, 3)), jnp.transpose(coords, (0, 2, 1, 3)), w_in,
        w_query, w_key, w_value, w_out, w_up, w_down,
    )
    return encoded.reshape(1, 1, rows, width)


def solution(mesh):
    in_specs = (
        P(("view", "seg"), None, None),
        P(("view", "seg"), None, None),
        P(("view", "seg"), None, None, None),
        P(("view", "seg"), None, None, None, None),
        P("view", "seg", None, None),
    ) + (P(),) * 7
    out_specs = P("view", "seg", None, None)
    return jax.shard_map(shards, mesh=mesh, in_specs=in_specs, out_specs=out_specs, check_vma=False)
```

profile of v0, /device:TPU:0, one launch (start us, length us, event | category | flops | bytes accessed | tf_op | source)
XLA Modules:
  0.0 75.7 jit_solution(2132123912577011537)
XLA Ops:
  0.0 73.6 %voxel_block.1 = bf16[512,768]{1,0:T(8,128)(2,1)} custom-call(bf16[1,1369,1024]{2,1,0:T(8,128)(2,1)} %features.1, s32[1,8,2,32]{3,2,1,0:T(2,128)} %patch_rows.1, s32[1,2,8]{2,1,0:T(2,128)} %bitcast.7, bf16[1,8,2,32,64]{4,3,2,1,0:T(8,128)(2,1)} %bitcast.5, s32[1,3,1,512]{3,2,1,0:T(1,128)} %bitcast.6, f32[1024,768]{1,0:T(8,128)} %w_in.1, ...), custom_call_target="tpu_custom_call" | custom-call | tf_op jit(solution)/shard_map/voxel_block/pallas_call | solution.py:398
  73.6 2.1 %copy.14 = bf16[1,1,512,768]{3,2,1,0:T(8,128)(2,1)} copy(bf16[1,1,512,768]{3,2,1,0:T(8,128)(2,1)} %bitcast.4) | data formatting | bytes 1572864
where the time goes:
time: 75.8 us; the launch traced here: 75.7 us
  Pallas kernels  73.6 us (97%)
  local copies, waits for them, and re-layouts  2.06 us (3%)
    pallas_call x1, Pallas kernels, shards(): pl.pallas_call(functools.partial(whole_kernel, V, G, (KS, bp, blk, QB, CC...  73.6 us
    unnamed x1, local copies, waits for them, and re-layouts  2.06 us

commit v1 on v0

--- a/solution.py
+++ b/solution.py
@@ -14,7 +14,7 @@
 BF16 = jnp.bfloat16
 CW = 128
 ID_ROWS = 16
-FF_STEP = 512
+FF_STEP = 768
 VMEM_LIMIT = 56 * 1024 * 1024
 
 
@@ -272,13 +272,11 @@
             for cc in range(CC):
                 view_copy(other, cc, 1, other).wait_recv()
                 early = product(1, me_v, cc) + product(1, other, cc)
+                most = product(0, me_v, cc) + product(0, outer_of, cc) + product(0, other, cc)
                 view_copy(far, cc, 2, other).wait_recv()
                 sums_out[cc] = (early + product(1, far, cc)).astype(BF16)
                 sum_copy(cc).start()
-                summed = (
-                    product(0, me_v, cc) + product(0, outer_of, cc)
-                    + product(0, other, cc) + product(0, far, cc)
-                )
+                summed = most + product(0, far, cc)
                 finish(cc, summed, tally)
             for cc in order:
                 view_copy(me_v, cc, 1, other).wait_send()
@@ -368,9 +366,9 @@
             if i > 0:
                 down(i - 1)
             hidden[i % 2] = jax.nn.gelu(up, approximate=True).astype(BF16)
-        encoded[...] = (stream[...] + jnp.dot(
+        encoded[...] = stream[...] + jnp.dot(
             hidden[(count - 1) % 2], vdown[(count - 1) * step:, :], preferred_element_type=F32
-        )).astype(BF16)
+        )
 
     extended = pltpu.VMEM((total, width), BF16)
     pl.run_scoped(
@@ -397,7 +395,7 @@
     dma = pltpu.SemaphoreType.DMA
     encoded = pl.pallas_call(
         functools.partial(whole_kernel, V, G, (KS, bp, blk, QB, CC)),
-        out_shape=jax.ShapeDtypeStruct((rows, width), BF16),
+        out_shape=jax.ShapeDtypeStruct((rows, width), F32),
         in_specs=[anyspace] + [vmem] * 4 + [anyspace] * 7,
         out_specs=vmem,
         scratch_shapes=[
@@ -434,7 +432,7 @@
         jnp.transpose(lift_weights, (0, 1, 2, 4, 3)), jnp.transpose(coords, (0, 2, 1, 3)), w_in,
         w_query, w_key, w_value, w_out, w_up, w_down,
     )
-    return encoded.reshape(1, 1, rows, width)
+    return encoded.astype(BF16).reshape(1, 1, rows, width)
 
 
 def solution(mesh):

time: 75.8 us -> 76.1 us (level)
  other arithmetic: 0 us -> 2.37 us
  local copies, waits for them, and re-layouts: 2.06 us -> 0 us
    reshape x0 -> x1, other arithmetic: none -> 2.37 us  [shards(): return encoded.astype(BF16).reshape(1, 1, rows, width)]
    unnamed x1 -> x0, local copies, waits for them, and re-layouts: 2.06 us -> none
where the time goes in v1:
time: 76.1 us; the launch traced here: 76 us
  Pallas kernels  73.6 us (97%)
  other arithmetic  2.37 us (3%)
    pallas_call x1, Pallas kernels, shards(): pl.pallas_call(functools.partial(whole_kernel, V, G, (KS, bp, blk, QB, CC...  73.6 us
    reshape x1, other arithmetic, shards(): return encoded.astype(BF16).reshape(1, 1, rows, width)  2.37 us

profile of v1, /device:TPU:0, one launch (start us, length us, event | category | flops | bytes accessed | tf_op | source)
XLA Modules:
  0.0 76.0 jit_solution(15802901234930546713)
XLA Ops:
  0.0 73.6 %voxel_block.1 = f32[512,768]{1,0:T(8,128)} custom-call(bf16[1,1369,1024]{2,1,0:T(8,128)(2,1)} %features.1, s32[1,8,2,32]{3,2,1,0:T(2,128)} %patch_rows.1, s32[1,2,8]{2,1,0:T(2,128)} %bitcast.7, bf16[1,8,2,32,64]{4,3,2,1,0:T(8,128)(2,1)} %bitcast.5, s32[1,3,1,512]{3,2,1,0:T(1,128)} %bitcast.6, f32[1024,768]{1,0:T(8,128)} %w_in.1, bf16[768,768]{1,0:T(8,128)(2,1)} %w_query.1, ...), custom_call_target="tpu_custom_call" | custom-call | tf_op jit(solution)/shard_map/voxel_block/pallas_call | solution.py:396
  73.6 2.4 %convert_bitcast_fusion = bf16[1,1,512,768]{3,2,1,0:T(8,128)(2,1)} fusion(f32[512,768]{1,0:T(8,128)} %voxel_block.1), kind=kLoop, calls=%fused_computation | loop fusion | flops 393216 | bytes 2359296 | tf_op jit(solution)/shard_map/reshape | solution.py:435
